TPU v7x, 256 devices: a whole 4x4x8 slice. The times are simulated.
256 devices in a mesh: ctx: 16 (over x, y_lo, core), exp: 16 (over y_hi, z).
Axes of the slice: x: 4, y: 4 (y_hi: 2, y_lo: 2; y = y_hi * 2 + y_lo), z: 8, core: 2. Of those that a mesh axis runs over, the one named last changes fastest.
Arguments:
- queries: bfloat16 [16, 2048, 1024], P('exp', 'ctx'), may hold values from -40 to 40
- keys: bfloat16 [16, 2048, 1024], P('exp', 'ctx'), may hold values from -6 to 6
- values: bfloat16 [16, 2048, 1024], P('exp', 'ctx'), may hold values from -6 to 6
- segments: int32 [16, 2048], P('exp'), may hold values from 0 to 7, never falling along the last dimension, each value on 1 to 1152 neighbouring positions
- hidden_state: bfloat16 [16, 2048, 2048], P('exp', 'ctx'), may hold values from -40 to 40
- norm_gain: float32 [2048], replicated, may hold values from 0.1 to 1.9
- route_gates: float32 [16, 2048, 2], P('exp', 'ctx'), may hold values from 0.2 to 1
- routes: int32 [16, 2048, 2], P('exp', 'ctx'), may hold values from 0 to 15, all different within a row; in each aligned block of 128 rows (0 to 127, 128 to 255, ..., all dimensions but the last counted through in order) at most 24 rows name the same one
- out_grad: bfloat16 [16, 2048, 2048], P('exp', 'ctx'), may hold values from -6 to 6
- w_gate: bfloat16 [16, 2048, 512], P('exp'), may hold values from -0.125 to 0.125
- w_up: bfloat16 [16, 2048, 512], P('exp'), may hold values from -0.125 to 0.125
- w_down: bfloat16 [16, 512, 2048], P('exp'), may hold values from -0.25 to 0.25
Outputs:
- query_grad: bfloat16 [16, 2048, 1024], P('exp', 'ctx')
- key_grad: bfloat16 [16, 2048, 1024], P('exp', 'ctx')
- value_grad: bfloat16 [16, 2048, 1024], P('exp', 'ctx')
- residual_grad: bfloat16 [16, 2048, 2048], P('exp', 'ctx')
Inputs may be any that keep to these rules, and one draw needn't show every extreme that they name: Among the frames of one device (aligned blocks of 128 frames) no expert is named by more than 24 routes, a bound that some block reaches; a frame names 2 different experts. `segments`: segment ids never fall along a sequence; a segment holds 1 to 1152 frames and one holds exactly 1152.
All inputs are finite; a program needn't handle non-finite values.
Results may differ from a plain program's by a relative error of at most 0.015.
Values may be sent and summed in bfloat16 or wider, within the bound.
No kernel may reach another device: no remote copies, remote signals or barrier semaphores. Data moves between devices by JAX's collectives and lax.ppermute only.
A program may use at most 128 MiB of HBM per device.

v0:
```python
import jax
import jax.numpy as jnp
from jax import lax
from jax.sharding import PartitionSpec as P

HEAD_DIM = 128
TOP = 2


EPSILON = 1e-06
MASKED = -1e30


def silu_parts(pre_act):
    sigmoid = jax.nn.sigmoid(pre_act)
    return (pre_act * sigmoid, sigmoid * (1.0 + pre_act * (1.0 - sigmoid)))


def expert_backward(normed_rows, scaled_rows, gate_mat, up_mat, down_mat):
    contract = (((1,), (1,)), ((), ()))
    gate_pre = jnp.dot(normed_rows, gate_mat, preferred_element_type=jnp.float32)
    up_pre = jnp.dot(normed_rows, up_mat, preferred_element_type=jnp.float32)
    hidden_grad = lax.dot_general(
        scaled_rows, down_mat, contract, preferred_element_type=jnp.float32
    )
    activated, slope = silu_parts(gate_pre)
    gate_grad = (hidden_grad * up_pre * slope).astype(jnp.bfloat16)
    up_grad = (hidden_grad * activated).astype(jnp.bfloat16)
    summed = lax.dot_general(gate_grad, gate_mat, contract, preferred_element_type=jnp.float32)
    summed = summed + lax.dot_general(up_grad, up_mat, contract, preferred_element_type=jnp.float32)
    return summed.astype(jnp.bfloat16)


def body(
    queries,
    keys,
    values,
    segments,
    hidden_state,
    norm_gain,
    route_gates,
    routes,
    out_grad,
    w_gate,
    w_up,
    w_down,
):
    tok_rows = hidden_state.shape[1]
    model_width = hidden_state.shape[2]
    expert_count = lax.axis_size("exp")
    capacity = 3 * tok_rows * TOP // (2 * expert_count)
    hidden_f = hidden_state[0].astype(jnp.float32)
    inverse = lax.rsqrt(jnp.mean(hidden_f * hidden_f, -1, keepdims=True) + EPSILON)
    normed = (hidden_f * inverse * norm_gain).astype(jnp.bfloat16)
    scaled = (route_gates[0][:, :, None] * out_grad[0][:, None, :].astype(jnp.float32)).astype(
        jnp.bfloat16
    )
    scaled = scaled.reshape(tok_rows * TOP, model_width)
    chosen = routes[0].reshape(tok_rows * TOP)
    onehot = (chosen[:, None] == jnp.arange(expert_count, dtype=jnp.int32)[None, :]).astype(
        jnp.int32
    )
    before = jnp.cumsum(onehot, 0) - onehot
    slot_index = jnp.sum(before * onehot, 1)
    target = chosen * capacity + slot_index
    source = (
        jnp.zeros((expert_count * capacity,), jnp.int32)
        .at[target]
        .set(jnp.arange(tok_rows * TOP, dtype=jnp.int32) + 1)
    )
    frame_slot = jnp.where(source > 0, (source - 1) // TOP + 1, 0)
    zero_row = jnp.zeros((1, model_width), jnp.bfloat16)
    send_normed = jnp.concatenate([zero_row, normed], 0)[frame_slot].reshape(
        expert_count, capacity, model_width
    )
    send_scaled = jnp.concatenate([zero_row, scaled], 0)[source].reshape(
        expert_count, capacity, model_width
    )
    gate_mat = w_gate[0]
    up_mat = w_up[0]
    down_mat = w_down[0]
    normed_in = lax.all_to_all(send_normed, "exp", split_axis=0, concat_axis=0, tiled=True)
    scaled_in = lax.all_to_all(send_scaled, "exp", split_axis=0, concat_axis=0, tiled=True)
    shape_in = normed_in.shape
    back = expert_backward(
        normed_in.reshape(-1, model_width),
        scaled_in.reshape(-1, model_width),
        gate_mat,
        up_mat,
        down_mat,
    ).reshape(shape_in)
    returned = lax.all_to_all(back, "exp", split_axis=0, concat_axis=0, tiled=True)
    per_route = returned.reshape(expert_count * capacity, model_width)[target].astype(jnp.float32)
    normed_grad = jnp.sum(per_route.reshape(tok_rows, TOP, model_width), 1)
    weighted = norm_gain * normed_grad
    residual = out_grad[0].astype(jnp.float32) + inverse * weighted
    residual = residual - hidden_f * inverse**3 * jnp.mean(hidden_f * weighted, -1, keepdims=True)
    residual_grad = residual.astype(jnp.bfloat16)
    att_width = queries.shape[2]
    head_count = att_width // HEAD_DIM
    inv_root = HEAD_DIM ** (-0.5)
    query_home = queries[0].reshape(tok_rows, head_count, HEAD_DIM)
    key_home = keys[0].reshape(tok_rows, head_count, HEAD_DIM)
    value_home = values[0].reshape(tok_rows, head_count, HEAD_DIM)
    grad_home = residual_grad[:, :att_width]
    grad_heads = grad_home.reshape(tok_rows, head_count, HEAD_DIM)
    seg_all = segments[0]
    seg_here = lax.dynamic_slice_in_dim(seg_all, lax.axis_index("ctx") * tok_rows, tok_rows)
    key_part = lax.all_gather(keys, "ctx", axis=1, tiled=True)
    value_part = lax.all_gather(values, "ctx", axis=1, tiled=True)
    count = key_part.shape[1]
    key_heads = key_part[0].reshape(count, head_count, HEAD_DIM)
    value_heads = value_part[0].reshape(count, head_count, HEAD_DIM)
    allowed = (seg_here[:, None] == seg_all[None, :])[None]
    scores = (
        jnp.einsum("qhd,khd->hqk", query_home, key_heads, preferred_element_type=jnp.float32)
        * inv_root
    )
    scores = jnp.where(allowed, scores, MASKED)
    row_peak = jnp.full((head_count, tok_rows), MASKED, jnp.float32)
    new_peak = jnp.maximum(row_peak, jnp.max(scores, -1))
    attend = jnp.where(allowed, jnp.exp(scores - new_peak[..., None]), 0.0)
    summed = jnp.sum(attend, -1)
    accum = jnp.einsum("hqk,khd->hqd", attend, value_heads, preferred_element_type=jnp.float32)
    row_peak, summed, accum = (new_peak, summed, accum)
    out = accum / summed[..., None]
    lse = row_peak + jnp.log(summed)
    delta = jnp.sum(jnp.transpose(grad_heads.astype(jnp.float32), (1, 0, 2)) * out, -1)
    lse_all, delta_all = (
        lax.all_gather(lse, "ctx", axis=1, tiled=True),
        lax.all_gather(delta, "ctx", axis=1, tiled=True),
    )
    grad_in = grad_home[None]
    query_part = lax.all_gather(queries, "ctx", axis=1, tiled=True)
    grad_part = lax.all_gather(grad_in, "ctx", axis=1, tiled=True)
    count = query_part.shape[1]
    query_heads = query_part[0].reshape(count, head_count, HEAD_DIM)
    grad_part_heads = grad_part[0].reshape(count, head_count, HEAD_DIM)
    allowed_rows = seg_all[:, None] == seg_here[None, :]
    scores = (
        jnp.einsum("qhd,khd->hqk", query_heads, key_home, preferred_element_type=jnp.float32)
        * inv_root
    )
    attend = jnp.where(allowed_rows[None], jnp.exp(scores - lse_all[..., None]), 0.0)
    attend_b = attend.astype(jnp.bfloat16)
    attend_grad = jnp.einsum(
        "qhd,khd->hqk", grad_part_heads, value_home, preferred_element_type=jnp.float32
    )
    score_grad = (attend * (attend_grad - delta_all[..., None])).astype(jnp.bfloat16)
    new_value = jnp.einsum(
        "hqk,qhd->khd", attend_b, grad_part_heads, preferred_element_type=jnp.float32
    )
    new_key = (
        jnp.einsum("hqk,qhd->khd", score_grad, query_heads, preferred_element_type=jnp.float32)
        * inv_root
    )
    query_part_grad = (
        jnp.einsum("hqk,khd->qhd", score_grad, key_home, preferred_element_type=jnp.float32)
        * inv_root
    )
    terms = query_part_grad.reshape(count, att_width)
    query_sum = lax.psum_scatter(terms.astype(jnp.bfloat16), "ctx", scatter_dimension=0, tiled=True)
    query_grad = query_sum[None]
    key_grad = new_key.reshape(tok_rows, att_width).astype(jnp.bfloat16)[None]
    value_grad = new_value.reshape(tok_rows, att_width).astype(jnp.bfloat16)[None]
    return (query_grad, key_grad, value_grad, residual_grad[None])


def solution(mesh):
    in_specs = (
        P("exp", "ctx", None),
        P("exp", "ctx", None),
        P("exp", "ctx", None),
        P("exp", None),
        P("exp", "ctx", None),
        P(),
        P("exp", "ctx", None),
        P("exp", "ctx", None),
        P("exp", "ctx", None),
        P("exp", None, None),
        P("exp", None, None),
        P("exp", None, None),
    )
    out_specs = (
        P("exp", "ctx", None),
        P("exp", "ctx", None),
        P("exp", "ctx", None),
        P("exp", "ctx", None),
    )
    return jax.shard_map(body, mesh=mesh, in_specs=in_specs, out_specs=out_specs, check_vma=False)
```

profile of v0, /device:TPU:32, one launch (start us, length us, event | category | flops | bytes accessed | tf_op | source)
XLA Modules:
  0.0 353.2 jit_solution(18435887810519471721)
XLA Ops:
  19.9 11.2 %all-to-all-start.1 = ((bf16[16,24,2048]{2,1,0:T(8,128)(2,1)}), bf16[16,24,2048]{2,1,0:T(8,128)(2,1)}, u32[]{:S(2)}, u32[]{:S(2)}) async-start(bf16[16,24,2048]{2,1,0:T(8,128)(2,1)} %bitcast.110), calls=%async_computation.1 | async-start | bytes 3145728 | tf_op jit(solution)/shard_map/all_to_all | solution.py:82
  37.1 3.7 %mul.181 = f32[256,2048]{1,0:T(8,128)} reshape(f32[128,2,2048]{2,1,0:T(2,128)} %mul.180) | data formatting | bytes 4194304 | tf_op jit(solution)/shard_map/mul | solution.py:55
  46.0 24.3 %all-to-all-done.1 = bf16[16,24,2048]{2,1,0:T(8,128)(2,1)} async-done(((bf16[16,24,2048]{2,1,0:T(8,128)(2,1)}), bf16[16,24,2048]{2,1,0:T(8,128)(2,1)}, u32[]{:S(2)}, u32[]{:S(2)}) %all-to-all-start.1) | async-done | bytes 1572896 | tf_op jit(solution)/shard_map/all_to_all | solution.py:82
  70.4 5.4 %all-to-all-start = ((bf16[16,24,2048]{2,1,0:T(8,128)(2,1)}), bf16[16,24,2048]{2,1,0:T(8,128)(2,1)}, u32[]{:S(2)}, u32[]{:S(2)}) async-start(bf16[16,24,2048]{2,1,0:T(8,128)(2,1)} %bitcast.111), calls=%async_computation | async-start | bytes 3145728 | tf_op jit(solution)/shard_map/all_to_all | solution.py:83
  79.7 35.2 %all-to-all-done = bf16[16,24,2048]{2,1,0:T(8,128)(2,1)} async-done(((bf16[16,24,2048]{2,1,0:T(8,128)(2,1)}), bf16[16,24,2048]{2,1,0:T(8,128)(2,1)}, u32[]{:S(2)}, u32[]{:S(2)}) %all-to-all-start) | async-done | bytes 1572896 | tf_op jit(solution)/shard_map/all_to_all | solution.py:83
  114.9 4.0 %fusion.23 = f32[384,512]{1,0:T(8,128)} fusion(bf16[384,2048]{1,0:T(8,128)(2,1)} %bitcast.10, bf16[1,512,2048]{2,1,0:T(8,128)(2,1)} %param.23), kind=kOutput, calls=%fused_computation.32 | convolution fusion | flops 805306368 | bytes 4456448 | tf_op jit(solution)/shard_map/dot_general | solution.py:23
  118.9 6.0 %fusion.16 = f32[384,2048]{1,0:T(8,128)} fusion(bf16[1,2048,512]{2,1,0:T(8,128)(2,1)} %param.21, f32[384,512]{1,0:T(8,128)} %fusion.23, bf16[384,2048]{1,0:T(8,128)(2,1)} %bitcast.13, bf16[1,2048,512]{2,1,0:T(8,128)(2,1)S(1)} %copy-done, f32[384,512]{1,0:T(8,128)S(1)} %fusion.18), kind=kOutput, calls=%fused_computation.25 | convolution fusion | flops 1612578816 | bytes 10485760 | tf_op jit(solution)/shard_map/dot_general | solution.py:29
  124.9 4.3 %add_convert_fusion = bf16[384,2048]{1,0:T(8,128)(2,1)} fusion(f32[384,2048]{1,0:T(8,128)} %fusion.16, bf16[1,2048,512]{2,1,0:T(8,128)(2,1)S(1)} %copy-done, f32[384,512]{1,0:T(8,128)} %fusion.23, f32[384,512]{1,0:T(8,128)S(1)} %fusion.18), kind=kOutput, calls=%fused_computation.24 | convolution fusion | flops 808058880 | bytes 8388608 | tf_op jit(solution)/shard_map/dot_general | solution.py:30
  129.2 5.3 %all-to-all-start.2 = ((bf16[16,24,2048]{2,1,0:T(8,128)(2,1)}), bf16[16,24,2048]{2,1,0:T(8,128)(2,1)S(1)}, u32[]{:S(2)}, u32[]{:S(2)}) async-start(bf16[16,24,2048]{2,1,0:T(8,128)(2,1)} %bitcast.109), calls=%async_computation.2 | async-start | bytes 3145728 | tf_op jit(solution)/shard_map/all_to_all | solution.py:92
  134.8 38.6 %all-to-all-done.2 = bf16[16,24,2048]{2,1,0:T(8,128)(2,1)S(1)} async-done(((bf16[16,24,2048]{2,1,0:T(8,128)(2,1)}), bf16[16,24,2048]{2,1,0:T(8,128)(2,1)S(1)}, u32[]{:S(2)}, u32[]{:S(2)}) %all-to-all-start.2) | async-done | bytes 1572896 | tf_op jit(solution)/shard_map/all_to_all | solution.py:92
  175.8 3.5 reshape.280
  179.3 4.2 %reduce_sum.62 = f32[128,2048]{1,0:T(8,128)S(1)} reduce(f32[128,2,2048]{2,1,0:T(2,128)} %reshape.280, f32[]{:T(128)} %constant.27.clone.1), dimensions={1}, to_apply=%region_7.8 | reduce | flops 262144 | bytes 3145732 | tf_op jit(solution)/shard_map/reduce_sum | solution.py:94
  187.6 6.5 %copy.64 = bf16[1,2048,1024]{1,2,0:T(8,128)(2,1)} copy(bf16[1,2048,1024]{2,1,0:T(8,128)(2,1)} %all-gather.10.cloned.1.call-done) | data formatting | bytes 8388608 | tf_op jit(solution)/shard_map/all_gather | solution.py:110
  194.1 4.3 %fusion = (f32[8,128]{1,0:T(8,128)S(1)}, f32[8,128,2048]{2,1,0:T(8,128)S(1)}) fusion(pred[128,2048]{1,0:T(8,128)(4,1)S(1)} %broadcast_compare_fusion, bf16[2048,8,128]{0,2,1:T(8,128)(2,1)} %bitcast.108, bf16[128,8,128]{2,1,0:T(8,128)(2,1)S(1)} %bitcast.119), kind=kOutput, calls=%fused_computation.9 | convolution fusion | flops 543161344 | bytes 13111296 | tf_op jit(solution)/shard_map/qhd,khd->hqk/dot_general | solution.py:116
  200.9 19.1 %all_gather.20 = f32[8,2048]{1,0:T(8,128)S(1)} all-gather(f32[8,128]{1,0:T(8,128)S(1)} %log_add_fusion), channel_id=1, replica_groups=mesh['ctx'=16,'exp'=16] {'ctx'}, dimensions={1}, use_global_device_ids=true | all-gather | bytes 69632 | tf_op jit(solution)/shard_map/all_gather | solution.py:130
  222.8 16.7 %all_gather.23 = f32[8,2048]{1,0:T(8,128)S(1)} all-gather(f32[8,128]{1,0:T(8,128)S(1)} %fusion.44), channel_id=1, replica_groups=mesh['ctx'=16,'exp'=16] {'ctx'}, dimensions={1}, use_global_device_ids=true | all-gather | bytes 69632 | tf_op jit(solution)/shard_map/all_gather | solution.py:131
  239.4 6.8 %fusion.76 = f32[8,2048,128]{2,1,0:T(8,128)} fusion(bf16[2048,8,128]{0,2,1:T(8,128)(2,1)} %bitcast.112, bf16[128,8,128]{0,2,1:T(8,128)(2,1)S(1)} %bitcast.114), kind=kOutput, calls=%fused_computation.117 | convolution fusion | flops 536870912 | bytes 12845056 | tf_op jit(solution)/shard_map/qhd,khd->hqk/dot_general | solution.py:141
  246.3 6.5 %copy.60 = bf16[2048,1024]{0,1:T(8,128)(2,1)} copy(bf16[2048,1024]{1,0:T(8,128)(2,1)} %all-gather.12.cloned.1.call-done) | data formatting | bytes 8388608 | tf_op jit(solution)/shard_map/all_gather | solution.py:135
  252.8 8.3 %multiply_convert_fusion.1 = bf16[8,2048,128]{2,1,0:T(8,128)(2,1)S(1)} fusion(f32[8,2048,128]{2,1,0:T(8,128)} %fusion.76, bf16[2048,8,128]{0,2,1:T(8,128)(2,1)} %bitcast.116, f32[8,2048]{1,0:T(8,128)S(1)} %all_gather.23, f32[8,2048]{1,0:T(8,128)S(1)} %all_gather.20, pred[2048,128]{1,0:T(8,128)(4,1)S(1)} %broadcast_compare_fusion.1, ...), kind=kOutput, calls=%fused_computation.5 | convolution fusion | flops 549453824 | bytes 17432576 | tf_op jit(solution)/shard_map/qhd,khd->hqk/dot_general | solution.py:146
  266.3 6.5 %copy.67 = bf16[2048,8,128]{0,2,1:T(8,128)(2,1)} copy(bf16[2048,8,128]{2,0,1:T(8,128)(2,1)} %fusion.15) | data formatting | bytes 8388608 | tf_op jit(solution)/shard_map/convert_element_type | solution.py:162
  272.8 6.4 %copy.75 = bf16[2048,1024]{1,0:T(8,128)(2,1)} copy(bf16[2048,1024]{0,1:T(8,128)(2,1)} %bitcast.107) | data formatting | bytes 8388608
  281.5 4.7 %fusion.34 = bf16[8,128,128]{1,2,0:T(8,128)(2,1)S(1)} fusion(bf16[2048,8,128]{0,2,1:T(8,128)(2,1)} %bitcast.113, bf16[8,2048,128]{2,1,0:T(8,128)(2,1)} %copy-done.7), kind=kOutput, calls=%fused_computation.43 | convolution fusion | flops 537133056 | bytes 8650752 | tf_op jit(solution)/shard_map/hqk,qhd->khd/dot_general | solution.py:154
  287.0 6.3 %fusion.35 = bf16[8,128,128]{2,1,0:T(8,128)(2,1)S(1)} fusion(bf16[2048,8,128]{0,2,1:T(8,128)(2,1)} %bitcast.117, f32[8,2048,128]{2,1,0:T(8,128)} %fusion.76, f32[8,2048]{1,0:T(8,128)S(1)} %all_gather.20, pred[2048,128]{1,0:T(8,128)(4,1)S(1)} %broadcast_compare_fusion.1), kind=kOutput, calls=%fused_computation.44 | convolution fusion | flops 545390592 | bytes 13172736 | tf_op jit(solution)/shard_map/hqk,qhd->khd/dot_general | solution.py:150
  294.2 50.5 %reduce-scatter.4.cloned.1.call-done = bf16[128,1024]{1,0:T(8,128)(2,1)} async-done(((bf16[2048,1024]{1,0:T(8,128)(2,1)}), bf16[128,1024]{1,0:T(8,128)(2,1)}) %reduce-scatter.4.cloned.1.call-update) | async-done | bytes 262160
  (97 shorter events, 50.7 us)
Async XLA Ops:
  7.2 111.7 %copy-start = (bf16[1,2048,512]{2,1,0:T(8,128)(2,1)S(1)}, bf16[1,2048,512]{2,1,0:T(8,128)(2,1)}, u32[]{:S(2)}) copy-start(bf16[1,2048,512]{2,1,0:T(8,128)(2,1)} %param.22) | copy-start | bytes 6291460
  7.2 180.4 %all-gather.10.cloned.1.call-start = ((), (), s32[]{:S(2)}) async-start(), calls=%async_computation.6 | async-start | bytes 4456448 | tf_op jit(solution)/shard_map/all_gather | solution.py:110
  7.9 186.2 %all-gather.8.cloned.1.call-start = ((), (), s32[]{:S(2)}) async-start(), calls=%async_computation.5 | async-start | bytes 4456448 | tf_op jit(solution)/shard_map/all_gather | solution.py:109
  16.8 14.4 %copy-start.14 = (f32[1,128,2]{1,2,0:T(2,128)S(1)}, f32[1,128,2]{1,2,0:T(2,128)}, u32[]{:S(2)}) copy-start(f32[1,128,2]{1,2,0:T(2,128)} %param.18) | copy-start | bytes 3076
  16.8 14.6 %copy-start.2 = (bf16[1,128,2048]{2,1,0:T(8,128)(2,1)S(1)}, bf16[1,128,2048]{2,1,0:T(8,128)(2,1)}, u32[]{:S(2)}) copy-start(bf16[1,128,2048]{2,1,0:T(8,128)(2,1)} %param.16) | copy-start | bytes 1572868
  19.9 50.4 %all-to-all-start.1 = ((bf16[16,24,2048]{2,1,0:T(8,128)(2,1)}), bf16[16,24,2048]{2,1,0:T(8,128)(2,1)}, u32[]{:S(2)}, u32[]{:S(2)}) async-start(bf16[16,24,2048]{2,1,0:T(8,128)(2,1)} %bitcast.110), calls=%async_computation.1 | async-start | bytes 3145728 | tf_op jit(solution)/shard_map/all_to_all | solution.py:82
  33.6 1.0 copy-start.4
  42.9 32.9 %copy-start.10 = (bf16[1,128,1024]{2,1,0:T(8,128)(2,1)S(1)}, bf16[1,128,1024]{2,1,0:T(8,128)(2,1)}, u32[]{:S(2)}) copy-start(bf16[1,128,1024]{2,1,0:T(8,128)(2,1)} %param.12) | copy-start | bytes 786436
  70.4 44.5 %all-to-all-start = ((bf16[16,24,2048]{2,1,0:T(8,128)(2,1)}), bf16[16,24,2048]{2,1,0:T(8,128)(2,1)}, u32[]{:S(2)}, u32[]{:S(2)}) async-start(bf16[16,24,2048]{2,1,0:T(8,128)(2,1)} %bitcast.111), calls=%async_computation | async-start | bytes 3145728 | tf_op jit(solution)/shard_map/all_to_all | solution.py:83
  75.7 163.7 %all-gather.6.cloned.1.call-start = ((), (), s32[]{:S(2)}) async-start(), calls=%async_computation.4 | async-start | bytes 4456448 | tf_op jit(solution)/shard_map/all_gather | solution.py:134
  129.2 44.2 %all-to-all-start.2 = ((bf16[16,24,2048]{2,1,0:T(8,128)(2,1)}), bf16[16,24,2048]{2,1,0:T(8,128)(2,1)S(1)}, u32[]{:S(2)}, u32[]{:S(2)}) async-start(bf16[16,24,2048]{2,1,0:T(8,128)(2,1)} %bitcast.109), calls=%async_computation.2 | async-start | bytes 3145728 | tf_op jit(solution)/shard_map/all_to_all | solution.py:92
  134.6 111.7 %all-gather.12.cloned.1.call-start = ((), (), s32[]{:S(2)}) async-start(), calls=%async_computation.7 | async-start | bytes 4456448 | tf_op jit(solution)/shard_map/all_gather | solution.py:135
  175.8 7.6 %copy-start.3 = (bf16[1,128,2048]{2,1,0:T(8,128)(2,1)S(1)}, bf16[1,128,2048]{2,1,0:T(8,128)(2,1)}, u32[]{:S(2)}) copy-start(bf16[1,128,2048]{2,1,0:T(8,128)(2,1)} %param.16) | copy-start | bytes 1572868
  175.8 7.7 %copy-start.12 = (f32[2048]{0:T(1024)S(1)}, f32[2048]{0:T(1024)}, u32[]{:S(2)}) copy-start(f32[2048]{0:T(1024)} %param.17) | copy-start | bytes 24580
  175.8 7.9 %copy-start.5 = (f32[128,2048]{1,0:T(8,128)S(1)}, f32[128,2048]{1,0:T(8,128)}, u32[]{:S(2)}) copy-start(f32[128,2048]{1,0:T(8,128)} %copy-done.4) | copy-start | bytes 3145732
  179.3 6.4 %copy-start.11 = (bf16[1,128,1024]{2,1,0:T(8,128)(2,1)S(1)}, bf16[1,128,1024]{2,1,0:T(8,128)(2,1)}, u32[]{:S(2)}) copy-start(bf16[1,128,1024]{2,1,0:T(8,128)(2,1)} %param.14) | copy-start | bytes 786436
  179.3 6.6 %copy-start.13 = (s32[1,2048]{1,0:T(1,128)S(1)}, s32[1,2048]{1,0:T(1,128)}, u32[]{:S(2)}) copy-start(s32[1,2048]{1,0:T(1,128)} %param.15) | copy-start | bytes 24580
  185.7 159.0 %reduce-scatter.4.cloned.1.call-start = ((), (), s32[]{:S(2)}) async-start(), calls=%async_computation.8 | async-start | bytes 4456448
  198.3 21.7 %copy-start.8 = (bf16[1,2048,1024]{1,2,0:T(8,128)(2,1)S(1)}, bf16[1,2048,1024]{1,2,0:T(8,128)(2,1)}, u32[]{:S(2)}) copy-start(bf16[1,2048,1024]{1,2,0:T(8,128)(2,1)} %copy.64) | copy-start | bytes 12582916
  220.0 19.4 %copy-start.6 = (bf16[1,128,1024]{1,2,0:T(8,128)(2,1)S(1)}, bf16[1,128,1024]{1,2,0:T(8,128)(2,1)}, u32[]{:S(2)}) copy-start(bf16[1,128,1024]{1,2,0:T(8,128)(2,1)} %copy.77) | copy-start | bytes 786436
  261.1 1.9 copy-start.7
  279.2 1.0 copy-start.9
  287.0 59.6 %copy-start.1 = (bf16[1,2048,512]{2,1,0:T(8,128)(2,1)S(1)}, bf16[1,2048,512]{2,1,0:T(8,128)(2,1)}, u32[]{:S(2)}) copy-start(bf16[1,2048,512]{2,1,0:T(8,128)(2,1)} %param.22) | copy-start | bytes 6291460
Sparse Core Ops, SparseCore 0:
  9.9 53.2 all-gather.9
  65.5 59.1 all-gather.7
  127.0 56.5 all-gather.5
  185.9 40.5 all-gather.11
  279.3 65.2 reduce-scatter.3
where the time goes:
time: 355 us; the launch traced here: 353 us
  waiting for transfers between devices  149 us (42%)
  local copies, waits for them, and re-layouts  59.3 us (17%)
  matrix products  53.8 us (15%)
  blocking collectives  35.8 us (10%)
  starting transfers between devices  22.3 us (6%)
  other arithmetic  18.5 us (5%)
  between operations  14.1 us (4%)
    unnamed x6, waiting for transfers between devices  51.2 us
    all_to_all x1, waiting for transfers between devices, body(): lax.all_to_all(back, 'exp', split_axis=0, concat_axis=0, tiled=True)  38.6 us
    all_to_all x1, waiting for transfers between devices, body(): lax.all_to_all(send_scaled, 'exp', split_axis=0, concat_axis=0, tiled=True)  35.2 us
    all_to_all x1, waiting for transfers between devices, body(): lax.all_to_all(send_normed, 'exp', split_axis=0, concat_axis=0, tiled=True)  24.3 us
    all_gather x1, blocking collectives, body(): lax.all_gather(lse, 'ctx', axis=1, tiled=True)  19.1 us
    all_gather x1, blocking collectives, body(): lax.all_gather(delta, 'ctx', axis=1, tiled=True)  16.7 us
    unnamed x40, local copies, waits for them, and re-layouts  15.9 us
    all_to_all x1, starting transfers between devices, body(): lax.all_to_all(send_normed, 'exp', split_axis=0, concat_axis=0, tiled=True)  11.2 us
  transfers between devices with their start and end apart: 8, of which 4 were waited for; matrix products, arithmetic and copies ran while one was open for 27% of the time, Pallas kernels for 0%

commit v1 on v0

v1 whole, which is shorter than its diff:
```python
import functools

import jax
import jax.numpy as jnp
from jax import lax
from jax.experimental import pallas as pl
from jax.experimental.pallas import tpu as pltpu
from jax.sharding import PartitionSpec as P

HEAD_DIM = 128
TOP = 2
EPSILON = 1e-06
MASKED = -1e30
LANES = 128
NT = (((1,), (1,)), ((), ()))
MIB = 1 << 20
VMEM = pltpu.MemorySpace.VMEM


def params(limit_mib, **more):
    return pltpu.CompilerParams(vmem_limit_bytes=limit_mib * MIB, **more)


def dot(a, b):
    return jnp.dot(a, b, preferred_element_type=jnp.float32)


def dot_nt(a, b):
    return lax.dot_general(a, b, NT, preferred_element_type=jnp.float32)


def three_parts(x):
    high = x.astype(jnp.bfloat16)
    rest = x - high.astype(jnp.float32)
    mid = rest.astype(jnp.bfloat16)
    low = (rest - mid.astype(jnp.float32)).astype(jnp.bfloat16)
    return high, mid, low


def pack_kernel(
    n_exp, capacity, steps, width,
    routes_ref, gates_ref, hidden_ref, gain_ref, out_grad_ref,
    send_ref, back_ref, inverse_ref,
    normed_scr, pick_scr, gate_scr,
):
    step = pl.program_id(0)
    rows = hidden_ref.shape[0]
    slots = n_exp * capacity

    @pl.when(step == 0)
    def _():
        hidden = hidden_ref[...].astype(jnp.float32)
        inverse = lax.rsqrt(jnp.mean(hidden * hidden, -1, keepdims=True) + EPSILON)
        normed_scr[...] = (hidden * inverse * gain_ref[...]).astype(jnp.bfloat16)
        inverse_ref[...] = jnp.broadcast_to(inverse, inverse_ref.shape)
        expert_id = lax.broadcasted_iota(jnp.int32, (n_exp, rows), 0)
        earlier = (
            lax.broadcasted_iota(jnp.int32, (rows, rows), 0)
            < lax.broadcasted_iota(jnp.int32, (rows, rows), 1)
        ).astype(jnp.bfloat16)
        slot_id = lax.broadcasted_iota(jnp.int32, (slots, rows), 0).astype(jnp.float32)
        first_slot = expert_id.astype(jnp.float32) * capacity
        total = None
        for j in range(TOP):
            named = (expert_id == routes_ref[j : j + 1, :]).astype(jnp.float32)
            place = first_slot + dot(named.astype(jnp.bfloat16), earlier)
            if j:
                place = place + used
            target = jnp.sum(named * place, 0, keepdims=True)
            pick = (slot_id == target).astype(jnp.float32)
            pick_scr[:, j * rows : (j + 1) * rows] = pick.astype(jnp.bfloat16)
            total = pick if total is None else total + pick
            if j == 0:
                used = jnp.sum(named, 1, keepdims=True)
            gate_scr[j] = jnp.broadcast_to(gates_ref[j : j + 1, :], (rows, rows)).T
        back_ref[...] = total.T.astype(jnp.bfloat16)

    @pl.when(step < steps)
    def _():
        columns = pl.ds(pl.multiple_of(step * width, width), width)
        part = normed_scr[:, columns]
        both = jnp.concatenate([part, part], 0)
        send_ref[...] = dot(pick_scr[...], both).astype(jnp.bfloat16)

    @pl.when(step >= steps)
    def _():
        columns = pl.ds(pl.multiple_of((step - steps) * width, width), width)
        part = out_grad_ref[:, columns].astype(jnp.float32)
        both = jnp.concatenate(
            [(gate_scr[j][:, :1] * part).astype(jnp.bfloat16) for j in range(TOP)], 0
        )
        send_ref[...] = dot(pick_scr[...], both).astype(jnp.bfloat16)


def pack(routes_t, gates_t, hidden, gain, out_grad, n_exp, capacity):
    rows, model = hidden.shape
    slots = n_exp * capacity
    width = 512
    steps = model // width
    whole = lambda shape: pl.BlockSpec(shape, lambda i: (0,) * len(shape))
    return pl.pallas_call(
        functools.partial(pack_kernel, n_exp, capacity, steps, width),
        grid=(2 * steps,),
        in_specs=[
            whole((TOP, rows)),
            whole((TOP, rows)),
            whole((rows, model)),
            whole((1, model)),
            whole((rows, model)),
        ],
        out_specs=[
            pl.BlockSpec((slots, width), lambda i: (0, i)),
            whole((rows, slots)),
            whole((rows, LANES)),
        ],
        out_shape=[
            jax.ShapeDtypeStruct((slots, 2 * model), jnp.bfloat16),
            jax.ShapeDtypeStruct((rows, slots), jnp.bfloat16),
            jax.ShapeDtypeStruct((rows, LANES), jnp.float32),
        ],
        scratch_shapes=[
            pltpu.VMEM((rows, model), jnp.bfloat16),
            pltpu.VMEM((slots, TOP * rows), jnp.bfloat16),
            pltpu.VMEM((TOP, rows, rows), jnp.float32),
        ],
        compiler_params=params(40),
        cost_estimate=pl.CostEstimate(
            flops=2 * slots * 4 * rows * model, bytes_accessed=8 * slots * model, transcendentals=0
        ),
        name="pack_rows",
    )(routes_t, gates_t, hidden, gain, out_grad)


def expert_kernel(
    model, front,
    rows_ref, gate_ref, up_ref, down_ref,
    front_ref, gate_grad_ref, up_grad_ref,
    total_scr, along_scr,
):
    step = pl.program_id(0)
    normed = rows_ref[:, :model]
    scaled = rows_ref[:, model:]
    gate_pre = dot(normed, gate_ref[...])
    up_pre = dot(normed, up_ref[...])
    hidden_grad = dot_nt(scaled, down_ref[...])
    sigmoid = jax.nn.sigmoid(gate_pre)
    slope = sigmoid * (1.0 + gate_pre * (1.0 - sigmoid))
    gate_grad = (hidden_grad * up_pre * slope).astype(jnp.bfloat16)
    up_grad = (hidden_grad * gate_pre * sigmoid).astype(jnp.bfloat16)
    gate_grad_ref[...] = gate_grad
    up_grad_ref[...] = up_grad
    along = jnp.sum(
        gate_grad.astype(jnp.float32) * gate_pre + up_grad.astype(jnp.float32) * up_pre,
        -1,
        keepdims=True,
    )
    part = dot_nt(gate_grad, gate_ref[:front, :]) + dot_nt(up_grad, up_ref[:front, :])

    @pl.when(step == 0)
    def _():
        total_scr[...] = part
        along_scr[...] = jnp.broadcast_to(along, along_scr.shape)

    @pl.when(step > 0)
    def _():
        total_scr[...] += part
        along_scr[...] += jnp.broadcast_to(along, along_scr.shape)

    @pl.when(step == pl.num_programs(0) - 1)
    def _():
        front_ref[:, :front] = total_scr[...].astype(jnp.bfloat16)
        whole = along_scr[...]
        high = whole.astype(jnp.bfloat16).astype(jnp.float32)
        lane = lax.broadcasted_iota(jnp.int32, whole.shape, 1)
        tail = jnp.where(lane == 0, high, jnp.where(lane == 1, whole - high, 0.0))
        front_ref[:, front:] = tail.astype(jnp.bfloat16)


def expert(rows, gate_mat, up_mat, down_mat, front):
    slots = rows.shape[0]
    model, units = gate_mat.shape
    chunk = 256
    return pl.pallas_call(
        functools.partial(expert_kernel, model, front),
        grid=(units // chunk,),
        in_specs=[
            pl.BlockSpec((slots, 2 * model), lambda i: (0, 0)),
            pl.BlockSpec((model, chunk), lambda i: (0, i)),
            pl.BlockSpec((model, chunk), lambda i: (0, i)),
            pl.BlockSpec((chunk, model), lambda i: (i, 0)),
        ],
        out_specs=[
            pl.BlockSpec((slots, front + LANES), lambda i: (0, 0)),
            pl.BlockSpec((slots, chunk), lambda i: (0, i)),
            pl.BlockSpec((slots, chunk), lambda i: (0, i)),
        ],
        out_shape=[
            jax.ShapeDtypeStruct((slots, front + LANES), jnp.bfloat16),
            jax.ShapeDtypeStruct((slots, units), jnp.bfloat16),
            jax.ShapeDtypeStruct((slots, units), jnp.bfloat16),
        ],
        scratch_shapes=[
            pltpu.VMEM((slots, front), jnp.float32),
            pltpu.VMEM((slots, LANES), jnp.float32),
        ],
        compiler_params=params(40),
        cost_estimate=pl.CostEstimate(
            flops=2 * slots * units * (3 * model + 2 * front),
            bytes_accessed=6 * model * units + 4 * slots * model,
            transcendentals=slots * units,
        ),
        name="expert_rows",
    )(rows, gate_mat, up_mat, down_mat)


def attend_kernel(
    scale, query_ref, key_ref, value_ref, here_ref, all_ref, out_ref, column_ref, row_ref
):
    count = key_ref.shape[0] * key_ref.shape[1]
    key = key_ref[...].reshape(count, HEAD_DIM)
    value = value_ref[...].reshape(count, HEAD_DIM)
    allowed = here_ref[:, :1] == all_ref[...]
    scores = jnp.where(allowed, dot_nt(query_ref[...], key) * scale, MASKED)
    peak = jnp.max(scores, -1, keepdims=True)
    attend = jnp.where(allowed, jnp.exp(scores - peak), 0.0)
    summed = jnp.sum(attend, -1, keepdims=True)
    out_ref[...] = dot(attend.astype(jnp.bfloat16), value) / summed
    lse = jnp.broadcast_to(peak + jnp.log(summed), column_ref.shape)
    column_ref[...] = lse
    row_ref[...] = lse.T[:8, :]


def attend_own(query, gathered, here, every, heads):
    rows = query.shape[0]
    n_ctx = gathered.shape[0]
    count = n_ctx * rows
    own = pl.BlockSpec((rows, HEAD_DIM), lambda h: (0, h))
    return pl.pallas_call(
        functools.partial(attend_kernel, HEAD_DIM ** (-0.5)),
        grid=(heads,),
        in_specs=[
            own,
            pl.BlockSpec((n_ctx, None, rows, HEAD_DIM), lambda h: (0, 0, 0, h)),
            pl.BlockSpec((n_ctx, None, rows, HEAD_DIM), lambda h: (0, 1, 0, h)),
            pl.BlockSpec((rows, LANES), lambda h: (0, 0)),
            pl.BlockSpec((1, count), lambda h: (0, 0)),
        ],
        out_specs=[own, own, pl.BlockSpec((None, 8, rows), lambda h: (h, 0, 0))],
        out_shape=[
            jax.ShapeDtypeStruct((rows, heads * HEAD_DIM), jnp.float32),
            jax.ShapeDtypeStruct((rows, heads * HEAD_DIM), jnp.float32),
            jax.ShapeDtypeStruct((heads, 8, rows), jnp.float32),
        ],
        compiler_params=params(40),
        cost_estimate=pl.CostEstimate(
            flops=4 * rows * count * heads * HEAD_DIM,
            bytes_accessed=4 * count * heads * HEAD_DIM,
            transcendentals=rows * count * heads,
        ),
        name="attend_own",
    )(query, gathered, gathered, here, every)


def front_kernel(
    model, heads,
    returned_ref, back_ref, hidden_ref, out_grad_ref, gain_ref, inverse_ref, out_ref, lse_ref,
    grad_ref, delta_ref, along_ref,
):
    front = heads * HEAD_DIM
    rows = hidden_ref.shape[0]
    inverse = inverse_ref[:, :1]
    sums = dot(back_ref[...], returned_ref[...])
    along = jnp.sum(sums[:, front:], -1, keepdims=True) * (1.0 / model)
    along_ref[...] = jnp.broadcast_to(along, along_ref.shape)
    weighted = gain_ref[...] * sums[:, :front]
    hidden = hidden_ref[...].astype(jnp.float32)
    residual = out_grad_ref[...].astype(jnp.float32) + inverse * weighted
    residual = residual - hidden * (inverse * inverse * along)
    grad = residual.astype(jnp.bfloat16)
    grad_ref[:rows, :] = grad
    product = grad.astype(jnp.float32) * out_ref[...]
    pad = jnp.zeros((grad_ref.shape[0] - rows - 6, rows), jnp.bfloat16)
    for h in range(heads):
        columns = slice(h * HEAD_DIM, (h + 1) * HEAD_DIM)
        delta = jnp.broadcast_to(jnp.sum(product[:, columns], -1, keepdims=True), (rows, rows))
        delta_ref[:, columns] = delta
        parts = three_parts(delta.T[:1, :]) + three_parts(lse_ref[h][:1, :])
        parts = [part.astype(jnp.float32) for part in parts] + [pad.astype(jnp.float32)]
        grad_ref[rows:, columns] = jnp.concatenate(parts, 0).astype(jnp.bfloat16)


def front_grad(returned, back, hidden, out_grad, gain, inverse, out, lse_rows, heads):
    rows, model = hidden.shape
    slots = back.shape[1]
    front = heads * HEAD_DIM
    extra = 16
    whole = lambda shape: pl.BlockSpec(shape, lambda i: (0,) * len(shape))
    return pl.pallas_call(
        functools.partial(front_kernel, model, heads),
        grid=(1,),
        in_specs=[
            whole((slots, front + LANES)),
            whole((rows, slots)),
            whole((rows, front)),
            whole((rows, front)),
            whole((1, front)),
            whole((rows, LANES)),
            whole((rows, front)),
            whole((heads, 8, rows)),
        ],
        out_specs=[whole((rows + extra, front)), whole((rows, front)), whole((rows, LANES))],
        out_shape=[
            jax.ShapeDtypeStruct((rows + extra, front), jnp.bfloat16),
            jax.ShapeDtypeStruct((rows, front), jnp.float32),
            jax.ShapeDtypeStruct((rows, LANES), jnp.float32),
        ],
        compiler_params=params(40),
        cost_estimate=pl.CostEstimate(
            flops=2 * slots * rows * front, bytes_accessed=6 * slots * front, transcendentals=0
        ),
        name="front_grad",
    )(returned, back, hidden, out_grad, gain, inverse, out, lse_rows)


def rest_kernel(
    front, returned_ref, back_ref, hidden_ref, out_grad_ref, gain_ref, inverse_ref, along_ref,
    grad_ref, residual_ref,
):
    rows = hidden_ref.shape[0]
    inverse = inverse_ref[:, :1]
    weighted = gain_ref[:, front:] * dot(back_ref[...], returned_ref[...])
    hidden = hidden_ref[:, front:].astype(jnp.float32)
    residual = out_grad_ref[:, front:].astype(jnp.float32) + inverse * weighted
    residual = residual - hidden * (inverse * inverse * along_ref[:, :1])
    residual_ref[:, front:] = residual.astype(jnp.bfloat16)
    residual_ref[:, :front] = grad_ref[:rows, :]


def rest_grad(returned, back, hidden, out_grad, gain, inverse, along, grad):
    rows, model = hidden.shape
    front = grad.shape[1]
    return pl.pallas_call(
        functools.partial(rest_kernel, front),
        out_shape=jax.ShapeDtypeStruct((rows, model), jnp.bfloat16),
        compiler_params=params(40),
        cost_estimate=pl.CostEstimate(
            flops=2 * back.shape[1] * rows * model, bytes_accessed=8 * rows * model, transcendentals=0
        ),
        name="rest_grad",
    )(returned, back, hidden, out_grad, gain, inverse, along, grad)


def query_kernel(
    scale, query_ref, grad_ref, key_ref, value_ref, here_ref, all_ref, lse_ref, delta_ref, result_ref
):
    count = key_ref.shape[0] * key_ref.shape[1]
    key = key_ref[...].reshape(count, HEAD_DIM)
    value = value_ref[...].reshape(count, HEAD_DIM)
    allowed = here_ref[:, :1] == all_ref[...]
    scores = dot_nt(query_ref[...], key) * scale
    attend = jnp.where(allowed, jnp.exp(scores - lse_ref[:, :1]), 0.0)
    attend_grad = dot_nt(grad_ref[...], value)
    score_grad = (attend * (attend_grad - delta_ref[:, :1])).astype(jnp.bfloat16)
    result_ref[...] = (dot(score_grad, key) * scale).astype(jnp.bfloat16)


def query_grads(query, grad, gathered, here, every, lse, delta, heads):
    rows = query.shape[0]
    n_ctx = gathered.shape[0]
    count = n_ctx * rows
    own = pl.BlockSpec((rows, HEAD_DIM), lambda h: (0, h))
    return pl.pallas_call(
        functools.partial(query_kernel, HEAD_DIM ** (-0.5)),
        grid=(heads,),
        in_specs=[
            own,
            own,
            pl.BlockSpec((n_ctx, None, rows, HEAD_DIM), lambda h: (0, 0, 0, h)),
            pl.BlockSpec((n_ctx, None, rows, HEAD_DIM), lambda h: (0, 1, 0, h)),
            pl.BlockSpec((rows, LANES), lambda h: (0, 0)),
            pl.BlockSpec((1, count), lambda h: (0, 0)),
            own,
            own,
        ],
        out_specs=own,
        out_shape=jax.ShapeDtypeStruct((rows, heads * HEAD_DIM), jnp.bfloat16),
        compiler_params=params(40),
        cost_estimate=pl.CostEstimate(
            flops=6 * rows * count * heads * HEAD_DIM,
            bytes_accessed=4 * count * heads * HEAD_DIM,
            transcendentals=rows * count * heads,
        ),
        name="query_grads",
    )(query, grad, gathered, gathered, here, every, lse, delta)


def key_kernel(
    scale, chunk, key_ref, value_ref, query_ref, grad_ref, here_ref, all_ref, key_out_ref, value_out_ref
):
    n_ctx, rows = query_ref.shape[0], query_ref.shape[1]
    key, value = key_ref[...], value_ref[...]
    here = here_ref[:, :1]
    key_sum = value_sum = 0.0
    for start in range(0, n_ctx, chunk):
        blocks = slice(start, start + chunk)
        query = query_ref[blocks].reshape(chunk * rows, HEAD_DIM)
        grad = grad_ref[blocks, :rows, :].reshape(chunk * rows, HEAD_DIM)
        delta, lse = [], []
        for b in range(start, start + chunk):
            extra = grad_ref[b, rows:, :].astype(jnp.float32)
            delta.append(extra[0:1] + extra[1:2] + extra[2:3])
            lse.append(extra[3:4] + extra[4:5] + extra[5:6])
        delta = jnp.concatenate(delta, 1)
        lse = jnp.concatenate(lse, 1)
        allowed = here == all_ref[:, start * rows : (start + chunk) * rows]
        scores = dot_nt(key, query) * scale
        attend = jnp.where(allowed, jnp.exp(scores - lse), 0.0)
        score_grad = (attend * (dot_nt(value, grad) - delta)).astype(jnp.bfloat16)
        value_sum += dot(attend.astype(jnp.bfloat16), grad)
        key_sum += dot(score_grad, query)
    key_out_ref[...] = (key_sum * scale).astype(jnp.bfloat16)
    value_out_ref[...] = value_sum.astype(jnp.bfloat16)


def key_grads(key, value, gathered, grads, here, every, heads):
    rows = key.shape[0]
    n_ctx = gathered.shape[0]
    count = n_ctx * rows
    own = pl.BlockSpec((rows, HEAD_DIM), lambda h: (0, h))
    return pl.pallas_call(
        functools.partial(key_kernel, HEAD_DIM ** (-0.5), 4),
        grid=(heads,),
        in_specs=[
            own,
            own,
            pl.BlockSpec((n_ctx, None, rows, HEAD_DIM), lambda h: (0, 2, 0, h)),
            pl.BlockSpec((n_ctx, grads.shape[1], HEAD_DIM), lambda h: (0, 0, h)),
            pl.BlockSpec((rows, LANES), lambda h: (0, 0)),
            pl.BlockSpec((1, count), lambda h: (0, 0)),
        ],
        out_specs=[own, own],
        out_shape=[jax.ShapeDtypeStruct((rows, heads * HEAD_DIM), jnp.bfloat16)] * 2,
        compiler_params=params(40),
        cost_estimate=pl.CostEstimate(
            flops=8 * rows * count * heads * HEAD_DIM,
            bytes_accessed=4 * count * heads * HEAD_DIM,
            transcendentals=rows * count * heads,
        ),
        name="key_grads",
    )(key, value, gathered, grads, here, every)


def body(
    queries, keys, values, segments, hidden_state, norm_gain,
    route_gates, routes, out_grad, w_gate, w_up, w_down,
):
    rows, model = hidden_state.shape[1:]
    front = queries.shape[2]
    heads = front // HEAD_DIM
    n_exp = lax.axis_size("exp")
    capacity = 3 * rows * TOP // (2 * n_exp)
    hidden, grad_in = hidden_state[0], out_grad[0]
    gain = norm_gain[None, :]
    query, key, value = queries[0], keys[0], values[0]
    gate_mat, up_mat, down_mat = w_gate[0], w_up[0], w_down[0]
    here = lax.dynamic_slice_in_dim(segments[0], lax.axis_index("ctx") * rows, rows)
    here = jnp.broadcast_to(here[:, None], (rows, LANES))

    def exchange(x):
        cut = x.reshape(n_exp, capacity, x.shape[1])
        return lax.all_to_all(cut, "exp", split_axis=0, concat_axis=0, tiled=True).reshape(x.shape)

    gathered = lax.all_gather(jnp.stack([key, value, query]), "ctx")
    send, back, inverse = pack(routes[0].T, route_gates[0].T, hidden, gain, grad_in, n_exp, capacity)
    arrived = exchange(send)
    first, gate_grad, up_grad = expert(arrived, gate_mat, up_mat, down_mat, front)
    first = exchange(first)
    second = dot_nt(gate_grad, gate_mat[front:]) + dot_nt(up_grad, up_mat[front:])
    second = second.astype(jnp.bfloat16)
    out, lse, lse_rows = attend_own(query, gathered, here, segments, heads)
    grad, delta, along = front_grad(
        first, back, hidden, grad_in, gain, inverse, out, lse_rows, heads
    )
    grads = lax.all_gather(grad, "ctx")
    second = exchange(second)
    query_grad = query_grads(query, grad, gathered, here, segments, lse, delta, heads)
    residual_grad = rest_grad(second, back, hidden, grad_in, gain, inverse, along, grad)
    key_grad, value_grad = key_grads(key, value, gathered, grads, here, segments, heads)
    return (query_grad[None], key_grad[None], value_grad[None], residual_grad[None])


def solution(mesh):
    rows = P("exp", "ctx", None)
    mats = P("exp", None, None)
    in_specs = (rows, rows, rows, P("exp", None), rows, P(), rows, rows, rows, mats, mats, mats)
    return jax.shard_map(
        body, mesh=mesh, in_specs=in_specs, out_specs=(rows,) * 4, check_vma=False
    )
```

time: 355 us -> 219 us (0.62)
  waiting for transfers between devices: 149 us -> 14.1 us
  blocking collectives: 35.8 us -> 121 us
  matrix products: 53.8 us -> 2.7 us
  local copies, waits for them, and re-layouts: 59.3 us -> 16.5 us
  Pallas kernels: 0 us -> 42.4 us
  starting transfers between devices: 22.3 us -> 5.5 us
  other arithmetic: 18.5 us -> 2.16 us
    all_to_all x0 -> x2, blocking collectives: none -> 121 us  [exchange(): lax.all_to_all(cut, 'exp', split_axis=0, concat_axis=0, tiled=True)]
    all_to_all x3 -> x1, waiting for transfers between devices: 98.2 us -> 0.01 us  [exchange(): lax.all_to_all(cut, 'exp', split_axis=0, concat_axis=0, tiled=True)]
    unnamed x6 -> x2, waiting for transfers between devices: 51.2 us -> 0.03 us
    dot_general x11 -> x2, matrix products: 53.8 us -> 2.7 us  [dot_nt(): return lax.dot_general(a, b, NT, preferred_element_type=jnp.float32)]
    pallas_call x0 -> x7, Pallas kernels: none -> 42.4 us  [the longest x1 11.2 us: key_grads(): pl.pallas_call(functools.partial(key_kernel, HEAD_DIM ** (-0.5), 4), grid...]
    all_gather x2 -> x0, blocking collectives: 35.8 us -> none  [the longest x1 19.1 us: body(): lax.all_gather(lse, 'ctx', axis=1, tiled=True)]
    all_to_all x3 -> x1, starting transfers between devices: 21.9 us -> 5.42 us  [exchange(): lax.all_to_all(cut, 'exp', split_axis=0, concat_axis=0, tiled=True)]
    all_gather x4 -> x2, waiting for transfers between devices: 0.03 us -> 14 us  [the longest x1 14 us: body(): gathered = lax.all_gather(jnp.stack([key, value, query]), 'ctx')]
  transfers between devices with their start and end apart: 8 -> 3, of which waited for: 4 -> 1; matrix products, arithmetic and copies ran while one was open for 27% -> 1% of each run, Pallas kernels for 0% -> 14%
where the time goes in v1:
time: 219 us
  blocking collectives  121 us (55%)
  Pallas kernels  42.4 us (19%)
  local copies, waits for them, and re-layouts  16.5 us (8%)
  between operations  14.3 us (7%)
  waiting for transfers between devices  14.1 us (6%)
  starting transfers between devices  5.5 us (3%)
  matrix products  2.7 us (1%)
    all_to_all x2, blocking collectives, exchange(): lax.all_to_all(cut, 'exp', split_axis=0, concat_axis=0, tiled=True)  121 us
    unnamed x46, local copies, waits for them, and re-layouts  16.5 us
    all_gather x1, waiting for transfers between devices, body(): gathered = lax.all_gather(jnp.stack([key, value, query]), 'ctx')  14 us
    pallas_call x1, Pallas kernels, key_grads(): pl.pallas_call(functools.partial(key_kernel, HEAD_DIM ** (-0.5), 4), grid...  11.2 us
    pallas_call x1, Pallas kernels, attend_own(): pl.pallas_call(functools.partial(attend_kernel, HEAD_DIM ** (-0.5)), grid...  8.99 us
    pallas_call x1, Pallas kernels, query_grads(): pl.pallas_call(functools.partial(query_kernel, HEAD_DIM ** (-0.5)), grid=...  8.39 us
    pallas_call x1, Pallas kernels, expert(): pl.pallas_call(functools.partial(expert_kernel, model, front), grid=(unit...  7.03 us
    all_to_all x1, starting transfers between devices, exchange(): lax.all_to_all(cut, 'exp', split_axis=0, concat_axis=0, tiled=True)  5.42 us
  transfers between devices with their start and end apart: 3, of which 1 were waited for; matrix products, arithmetic and copies ran while one was open for 1% of the time, Pallas kernels for 14%

profile of v1, /device:TPU:32, one launch (start us, length us, event | category | flops | bytes accessed | tf_op | source)
XLA Modules:
  0.0 218.7 jit_solution(15499765285840841126)
XLA Ops:
  7.3 2.2 pad_maximum_fusion
  9.5 3.1 %pack_rows.1 = (bf16[384,4096]{1,0:T(8,128)(2,1)S(1)}, bf16[128,384]{1,0:T(8,128)(2,1)S(1)}, f32[128,128]{1,0:T(8,128)S(1)}) custom-call(s32[2,128]{1,0:T(2,128)S(1)} %bitcast.63, f32[2,128]{1,0:T(2,128)S(1)} %bitcast.64, bf16[128,2048]{1,0:T(8,128)(2,1)S(1)} %bitcast.49, f32[1,2048]{1,0:T(1,128)S(1)} %bitcast.59, bf16[128,2048]{1,0:T(8,128)(2,1)S(1)} %bitcast.52), custom_call_target="tpu_custom_call" | custom-call | flops 805306368 | bytes 6291456 | tf_op jit(solution)/shard_map/pack_rows/pallas_call | solution.py:101
  12.7 83.8 %all_to_all.15 = bf16[16,24,4096]{2,1,0:T(8,128)(2,1)S(1)} all-to-all(bf16[16,24,4096]{2,1,0:T(8,128)(2,1)S(1)} %bitcast.45), channel_id=1, replica_groups=mesh['ctx'=16,'exp'=16] {'exp'}, dimensions={0} | all-to-all | bytes 6291456 | tf_op jit(solution)/shard_map/all_to_all | solution.py:471
  96.5 7.0 %expert_rows.1 = (bf16[384,1152]{1,0:T(8,128)(2,1)}, bf16[384,512]{1,0:T(8,128)(2,1)S(1)}, bf16[384,512]{1,0:T(8,128)(2,1)S(1)}) custom-call(bf16[384,4096]{1,0:T(8,128)(2,1)S(1)} %bitcast.44, bf16[2048,512]{1,0:T(8,128)(2,1)S(1)} %bitcast.57, bf16[2048,512]{1,0:T(8,128)(2,1)S(1)} %bitcast.58, bf16[512,2048]{1,0:T(8,128)(2,1)S(1)} %bitcast.62), custom_call_target="tpu_custom_call" | custom-call | flops 3221225472 | bytes 9437184 | tf_op jit(solution)/shard_map/expert_rows/pallas_call | solution.py:183
  103.6 0.8 copy-done.13
  104.3 0.7 copy-done.15
  105.0 5.4 %all-to-all-start.1 = ((bf16[16,24,1152]{2,1,0:T(8,128)(2,1)}), bf16[16,24,1152]{2,1,0:T(8,128)(2,1)S(1)}, u32[]{:S(2)}, u32[]{:S(2)}) async-start(bf16[16,24,1152]{2,1,0:T(8,128)(2,1)} %bitcast.13), calls=%async_computation.1 | async-start | bytes 1769472 | tf_op jit(solution)/shard_map/all_to_all | solution.py:471
  110.5 14.0 %all-gather.5.cloned.1.call-done = bf16[48,128,1024]{2,1,0:T(8,128)(2,1)} async-done(((bf16[3,128,1024]{2,1,0:T(8,128)(2,1)}), bf16[48,128,1024]{2,1,0:T(8,128)(2,1)}) %all-gather.5.cloned.1.call-update) | async-done | bytes 12582928 | tf_op jit(solution)/shard_map/all_gather | solution.py:473
  124.6 0.1 broadcast_in_dim.25.here_ref
  124.7 4.6 %copy-done = bf16[48,128,1024]{2,1,0:T(8,128)(2,1)S(1)} copy-done((bf16[48,128,1024]{2,1,0:T(8,128)(2,1)S(1)}, bf16[48,128,1024]{2,1,0:T(8,128)(2,1)}, u32[]{:S(2)}) %copy-start) | copy-done | bytes 12582936
  129.3 9.0 %attend_own.1 = (f32[128,1024]{1,0:T(8,128)S(1)}, f32[128,1024]{1,0:T(8,128)S(1)}, f32[8,8,128]{2,1,0:T(8,128)S(1)}) custom-call(bf16[128,1024]{1,0:T(8,128)(2,1)S(1)} %bitcast.47, bf16[16,3,128,1024]{3,2,1,0:T(8,128)(2,1)S(1)} %bitcast.38, bf16[16,3,128,1024]{3,2,1,0:T(8,128)(2,1)S(1)} %bitcast.39, s32[128,128]{1,0:T(8,128)S(1)} %broadcast_in_dim.25.here_ref, ...), custom_call_target="tpu_custom_call" | custom-call | flops 1073741824 | bytes 8388608 | tf_op jit(solution)/shard_map/attend_own/pallas_call | solution.py:238
  138.3 0.8 copy-done.11
  139.1 0.6 copy-done.18
  139.7 1.0 copy-done.12
  140.7 0.8 copy-done.19
  141.5 1.5 front_grad.1
  143.0 2.1 fusion.1
  145.2 0.6 add_convert_fusion
  145.8 37.1 %all_to_all.16 = bf16[16,24,1024]{2,1,0:T(8,128)(2,1)S(1)} all-to-all(bf16[16,24,1024]{2,1,0:T(8,128)(2,1)S(1)} %bitcast.65), channel_id=1, replica_groups=mesh['ctx'=16,'exp'=16] {'exp'}, dimensions={0} | all-to-all | bytes 1572864 | tf_op jit(solution)/shard_map/all_to_all | solution.py:471
  182.9 2.1 rest_grad.1
  185.1 4.8 %copy-done.1 = bf16[48,128,1024]{2,1,0:T(8,128)(2,1)S(1)} copy-done((bf16[48,128,1024]{2,1,0:T(8,128)(2,1)S(1)}, bf16[48,128,1024]{2,1,0:T(8,128)(2,1)}, u32[]{:S(2)}) %copy-start.1) | copy-done | bytes 12582936
  189.8 8.4 %query_grads.1 = bf16[128,1024]{1,0:T(8,128)(2,1)} custom-call(bf16[128,1024]{1,0:T(8,128)(2,1)S(1)} %bitcast.48, bf16[144,1024]{1,0:T(8,128)(2,1)} %get-tuple-element.24.grad_ref, bf16[16,3,128,1024]{3,2,1,0:T(8,128)(2,1)S(1)} %bitcast.40, bf16[16,3,128,1024]{3,2,1,0:T(8,128)(2,1)S(1)} %bitcast.41, s32[128,128]{1,0:T(8,128)S(1)} %broadcast_in_dim.25.here_ref, ...), custom_call_target="tpu_custom_call" | custom-call | flops 1610612736 | bytes 8388608 | tf_op jit(solution)/shard_map/query_grads/pallas_call | solution.py:372
  198.3 2.3 %copy-done.2 = bf16[2304,1024]{1,0:T(8,128)(2,1)S(1)} copy-done((bf16[2304,1024]{1,0:T(8,128)(2,1)S(1)}, bf16[2304,1024]{1,0:T(8,128)(2,1)}, u32[]{:S(2)}) %copy-start.2) | copy-done | bytes 4718616
  200.6 11.2 %key_grads.1 = (bf16[128,1024]{1,0:T(8,128)(2,1)}, bf16[128,1024]{1,0:T(8,128)(2,1)}) custom-call(bf16[128,1024]{1,0:T(8,128)(2,1)S(1)} %bitcast.56, bf16[128,1024]{1,0:T(8,128)(2,1)S(1)} %bitcast.55, bf16[16,3,128,1024]{3,2,1,0:T(8,128)(2,1)} %bitcast.37, bf16[16,144,1024]{2,1,0:T(8,128)(2,1)S(1)} %bitcast.42, s32[128,128]{1,0:T(8,128)S(1)} %broadcast_in_dim.25.here_ref, ...), custom_call_target="tpu_custom_call" | custom-call | flops 2147483648 | bytes 8388608 | tf_op jit(solution)/shard_map/key_grads/pallas_call | solution.py:430
  (44 shorter events, 0.2 us)
Async XLA Ops:
  7.2 2.3 %copy-start.21 = (s32[1,128,2]{1,2,0:T(2,128)S(1)}, s32[1,128,2]{1,2,0:T(2,128)}, u32[]{:S(2)}) copy-start(s32[1,128,2]{1,2,0:T(2,128)} %param.19) | copy-start | bytes 3076
  7.2 2.3 %copy-start.22 = (f32[1,128,2]{1,2,0:T(2,128)S(1)}, f32[1,128,2]{1,2,0:T(2,128)}, u32[]{:S(2)}) copy-start(f32[1,128,2]{1,2,0:T(2,128)} %param.18) | copy-start | bytes 3076
  7.2 2.3 %copy-start.4 = (bf16[1,128,2048]{2,1,0:T(8,128)(2,1)S(1)}, bf16[1,128,2048]{2,1,0:T(8,128)(2,1)}, u32[]{:S(2)}) copy-start(bf16[1,128,2048]{2,1,0:T(8,128)(2,1)} %param.16) | copy-start | bytes 1572868
  7.2 2.3 %copy-start.17 = (f32[2048]{0:T(1024)S(1)}, f32[2048]{0:T(1024)}, u32[]{:S(2)}) copy-start(f32[2048]{0:T(1024)} %param.17) | copy-start | bytes 24580
  7.2 2.3 %copy-start.5 = (bf16[1,128,2048]{2,1,0:T(8,128)(2,1)S(1)}, bf16[1,128,2048]{2,1,0:T(8,128)(2,1)}, u32[]{:S(2)}) copy-start(bf16[1,128,2048]{2,1,0:T(8,128)(2,1)} %param.20) | copy-start | bytes 1572868
  7.2 117.4 %all-gather.5.cloned.1.call-start = ((), (), s32[]{:S(2)}) async-start(), calls=%async_computation.3 | async-start | bytes 13369344 | tf_op jit(solution)/shard_map/all_gather | solution.py:473
  12.7 83.8 %copy-start.8 = (bf16[1,2048,512]{2,1,0:T(8,128)(2,1)S(1)}, bf16[1,2048,512]{2,1,0:T(8,128)(2,1)}, u32[]{:S(2)}) copy-start(bf16[1,2048,512]{2,1,0:T(8,128)(2,1)} %param.21) | copy-start | bytes 6291460
  12.7 83.8 %copy-start.9 = (bf16[1,2048,512]{2,1,0:T(8,128)(2,1)S(1)}, bf16[1,2048,512]{2,1,0:T(8,128)(2,1)}, u32[]{:S(2)}) copy-start(bf16[1,2048,512]{2,1,0:T(8,128)(2,1)} %param.22) | copy-start | bytes 6291460
  12.7 83.8 %copy-start.20 = (bf16[1,512,2048]{2,1,0:T(8,128)(2,1)S(1)}, bf16[1,512,2048]{2,1,0:T(8,128)(2,1)}, u32[]{:S(2)}) copy-start(bf16[1,512,2048]{2,1,0:T(8,128)(2,1)} %param.23) | copy-start | bytes 6291460
  96.5 14.0 %copy-start.16 = (s32[1,2048]{1,0:T(1,128)S(1)}, s32[1,2048]{1,0:T(1,128)}, u32[]{:S(2)}) copy-start(s32[1,2048]{1,0:T(1,128)} %all_ref.5) | copy-start | bytes 24580
  96.5 28.2 %copy-start.3 = (bf16[1,128,1024]{2,1,0:T(8,128)(2,1)S(1)}, bf16[1,128,1024]{2,1,0:T(8,128)(2,1)}, u32[]{:S(2)}) copy-start(bf16[1,128,1024]{2,1,0:T(8,128)(2,1)} %param.12) | copy-start | bytes 786436
  103.5 0.8 copy-start.13
  105.0 34.6 %all-to-all-start.1 = ((bf16[16,24,1152]{2,1,0:T(8,128)(2,1)}), bf16[16,24,1152]{2,1,0:T(8,128)(2,1)S(1)}, u32[]{:S(2)}, u32[]{:S(2)}) async-start(bf16[16,24,1152]{2,1,0:T(8,128)(2,1)} %bitcast.13), calls=%async_computation.1 | async-start | bytes 1769472 | tf_op jit(solution)/shard_map/all_to_all | solution.py:471
  110.5 87.8 %all-gather.7.cloned.1.call-start = ((), (), s32[]{:S(2)}) async-start(), calls=%async_computation.4 | async-start | bytes 5013504 | tf_op jit(solution)/shard_map/all_gather | solution.py:484
  124.7 4.6 %copy-start = (bf16[48,128,1024]{2,1,0:T(8,128)(2,1)S(1)}, bf16[48,128,1024]{2,1,0:T(8,128)(2,1)}, u32[]{:S(2)}) copy-start(bf16[48,128,1024]{2,1,0:T(8,128)(2,1)} %all-gather.5.cloned.1.call-done) | copy-start | bytes 37748740
  138.3 0.8 copy-start.11
  139.7 1.0 copy-start.12
  140.7 0.8 copy-start.19
  143.0 2.1 copy-start.14
  143.0 2.1 copy-start.10
  185.1 4.8 %copy-start.1 = (bf16[48,128,1024]{2,1,0:T(8,128)(2,1)S(1)}, bf16[48,128,1024]{2,1,0:T(8,128)(2,1)}, u32[]{:S(2)}) copy-start(bf16[48,128,1024]{2,1,0:T(8,128)(2,1)} %all-gather.5.cloned.1.call-done) | copy-start | bytes 37748740
  189.8 8.4 %copy-start.6 = (bf16[1,128,1024]{2,1,0:T(8,128)(2,1)S(1)}, bf16[1,128,1024]{2,1,0:T(8,128)(2,1)}, u32[]{:S(2)}) copy-start(bf16[1,128,1024]{2,1,0:T(8,128)(2,1)} %param.14) | copy-start | bytes 786436
  189.8 8.4 %copy-start.7 = (bf16[1,128,1024]{2,1,0:T(8,128)(2,1)S(1)}, bf16[1,128,1024]{2,1,0:T(8,128)(2,1)}, u32[]{:S(2)}) copy-start(bf16[1,128,1024]{2,1,0:T(8,128)(2,1)} %param.13) | copy-start | bytes 786436
  198.2 2.3 %copy-start.2 = (bf16[2304,1024]{1,0:T(8,128)(2,1)S(1)}, bf16[2304,1024]{1,0:T(8,128)(2,1)}, u32[]{:S(2)}) copy-start(bf16[2304,1024]{1,0:T(8,128)(2,1)} %all-gather.7.cloned.1.call-done) | copy-start | bytes 14155780
  (2 other events, 1.4 us)
Sparse Core Ops, SparseCore 0:
  9.9 114.6 all-gather.4
  143.1 51.5 all-gather.6
